TPU v7x, 32 devices: a whole 2x2x4 slice. The times are simulated.
32 devices in a mesh: seq: 4 (over y, x), shard: 8 (over z, core).
Axes of the slice: x: 2, y: 2, z: 4, core: 2. Of those that a mesh axis runs over, the one named last changes fastest.
Arguments:
- hidden_in: bfloat16 [16, 2048, 768], P('shard', 'seq'), may hold values from -6 to 6
- seq_lengths: int32 [16], P('shard'), may hold values from 1 to 2048, as said below
- w_qkv: bfloat16 [768, 2304], P('shard'), may hold values from -0.21875 to 0.21875
- b_query: bfloat16 [768], P('shard'), may hold values from -1.5 to 1.5
- b_value: bfloat16 [768], P('shard'), may hold values from -0.5 to 0.5
- w_out: bfloat16 [768, 768], P('shard'), may hold values from -6 to 6
- b_out: bfloat16 [768], P('shard'), may hold values from -1 to 1
- ln1_gain: bfloat16 [768], P('shard'), may hold values from 0.5 to 1.5
- ln1_bias: bfloat16 [768], P('shard'), may hold values from -1 to 1
- w_up: bfloat16 [768, 3072], P('shard'), may hold values from -0.21875 to 0.21875
- b_up: bfloat16 [3072], P('shard'), may hold values from -1 to 1
- w_down: bfloat16 [3072, 768], P('shard'), may hold values from -0.109375 to 0.109375
- b_down: bfloat16 [768], P('shard'), may hold values from -1 to 1
- ln2_gain: bfloat16 [768], P('shard'), may hold values from 0.5 to 1.5
- ln2_bias: bfloat16 [768], P('shard'), may hold values from -1 to 1
- cotangent: bfloat16 [16, 2048, 768], P('shard', 'seq'), may hold values from -6 to 6
Outputs:
- output: bfloat16 [16, 2048, 768], P('shard', 'seq')
- grad_input: bfloat16 [16, 2048, 768], P('shard', 'seq')
- grad_w_qkv: float32 [768, 2304], P('shard')
- grad_b_query: float32 [768], P('shard')
- grad_b_value: float32 [768], P('shard')
- grad_w_out: float32 [768, 768], P('shard')
- grad_b_out: float32 [768], P('shard')
- grad_ln1_gain: float32 [768], P('shard')
- grad_ln1_bias: float32 [768], P('shard')
- grad_w_up: float32 [768, 3072], P('shard')
- grad_b_up: float32 [3072], P('shard')
- grad_w_down: float32 [3072, 768], P('shard')
- grad_b_down: float32 [768], P('shard')
- grad_ln2_gain: float32 [768], P('shard')
- grad_ln2_bias: float32 [768], P('shard')
Inputs may be any that keep to these rules, and one draw needn't show every extreme that they name: `seq_lengths`: of sequences 2 i and 2 i + 1, at least one has all 2048 positions valid.
All inputs are finite; a program needn't handle non-finite values.
Results may differ from a plain program's by a relative error of at most 0.018.
Values may be sent and summed in bfloat16 or wider, within the bound.
A program may use at most 192 MiB of HBM per device.

v0:
```python
import jax
import jax.numpy as jnp
from jax import lax
from jax.sharding import PartitionSpec as P

DH = 64
EPS = 1e-12
NEG_FILL = -1e30
HALF_ROOT = 0.7071067811865476
INV_ROOT_TAU = 0.3989422804014327


def dot_rows(left_op, right_op):
    return lax.dot_general(
        left_op, right_op, (((0,), (0,)), ((), ())), preferred_element_type=jnp.float32
    )


def dot_last(left_op, right_op):
    return lax.dot_general(
        left_op, right_op, (((1,), (1,)), ((), ())), preferred_element_type=jnp.float32
    )


def owner_order(grad_arr, shard_count, group_count):
    rows = grad_arr.shape[0]
    piece = rows // (shard_count * group_count)
    rest = grad_arr.shape[1:]
    split = grad_arr.reshape((shard_count, group_count, piece) + rest)
    return jnp.swapaxes(split, 0, 1).reshape(grad_arr.shape)


def reorder_all(grad_list, shard_count, group_count):
    return tuple((owner_order(grad_arr, shard_count, group_count) for grad_arr in grad_list))


def norm_forward(hidden, gain_vec, shift_vec):
    mean_val = jnp.mean(hidden, axis=-1, keepdims=True)
    centered = hidden - mean_val
    inv_std = lax.rsqrt(jnp.mean(centered * centered, axis=-1, keepdims=True) + EPS)
    normed = centered * inv_std
    return (normed * gain_vec + shift_vec, normed, inv_std)


def norm_backward(grad_out, normed, inv_std, gain_vec):
    grad_gain = jnp.sum(grad_out * normed, axis=0)
    grad_shift = jnp.sum(grad_out, axis=0)
    scaled = grad_out * gain_vec
    grad_in = inv_std * (
        scaled
        - jnp.mean(scaled, axis=-1, keepdims=True)
        - normed * jnp.mean(scaled * normed, axis=-1, keepdims=True)
    )
    return (grad_in, grad_gain, grad_shift)


def gelu_parts(pre_act):
    cdf_val = 0.5 * (1.0 + lax.erf(pre_act * HALF_ROOT))
    pdf_val = jnp.exp(-0.5 * pre_act * pre_act) * INV_ROOT_TAU
    return (pre_act * cdf_val, cdf_val + pre_act * pdf_val)


def masked_scores(query_blk, keys_all, key_valid, scale_val):
    scores = (
        jnp.einsum("bhd,khd->hbk", query_blk, keys_all, preferred_element_type=jnp.float32)
        * scale_val
    )
    return jnp.where(key_valid[None, None, :], scores, NEG_FILL)


def attend_forward(head_data, length, block_rows):
    seq_len = head_data.shape[0]
    heads_here = head_data.shape[2]
    head_size = head_data.shape[3]
    keys_all = head_data[:, 1]
    values_all = head_data[:, 2]
    key_valid = jnp.arange(seq_len) < length
    scale_val = head_size ** (-0.5)
    query_blocks = head_data[:, 0].reshape(seq_len // block_rows, block_rows, heads_here, head_size)

    def one_block(query_blk):
        scores = masked_scores(query_blk, keys_all, key_valid, scale_val)
        row_max = jnp.max(scores, axis=-1, keepdims=True)
        exp_scores = jnp.exp(scores - row_max)
        row_sum = jnp.sum(exp_scores, axis=-1, keepdims=True)
        attn_prob = (exp_scores / row_sum).astype(jnp.bfloat16)
        out_blk = jnp.einsum(
            "hbk,khd->bhd", attn_prob, values_all, preferred_element_type=jnp.float32
        )
        return (out_blk, (row_max + jnp.log(row_sum))[..., 0])

    out_blocks, row_lse = lax.map(one_block, query_blocks)
    return (out_blocks.reshape(seq_len, heads_here, head_size), row_lse)


def attend_backward(head_data, grad_att, row_lse, length, block_rows):
    seq_len = head_data.shape[0]
    heads_here = head_data.shape[2]
    head_size = head_data.shape[3]
    keys_all = head_data[:, 1]
    values_all = head_data[:, 2]
    key_valid = jnp.arange(seq_len) < length
    scale_val = head_size ** (-0.5)
    block_count = seq_len // block_rows
    query_blocks = head_data[:, 0].reshape(block_count, block_rows, heads_here, head_size)
    grad_blocks = grad_att.reshape(block_count, block_rows, heads_here, head_size)

    def one_block(carried, pieces):
        grad_keys, grad_values = carried
        query_blk, grad_blk, lse_blk = pieces
        scores = masked_scores(query_blk, keys_all, key_valid, scale_val)
        attn_prob = jnp.exp(scores - lse_blk[..., None])
        grad_prob = jnp.einsum(
            "bhd,khd->hbk", grad_blk, values_all, preferred_element_type=jnp.float32
        )
        row_dot = jnp.sum(grad_prob * attn_prob, axis=-1, keepdims=True)
        grad_scores = (attn_prob * (grad_prob - row_dot)).astype(jnp.bfloat16)
        grad_query = (
            jnp.einsum("hbk,khd->bhd", grad_scores, keys_all, preferred_element_type=jnp.float32)
            * scale_val
        )
        grad_keys = (
            grad_keys
            + jnp.einsum("hbk,bhd->khd", grad_scores, query_blk, preferred_element_type=jnp.float32)
            * scale_val
        )
        grad_values = grad_values + jnp.einsum(
            "hbk,bhd->khd",
            attn_prob.astype(jnp.bfloat16),
            grad_blk,
            preferred_element_type=jnp.float32,
        )
        return ((grad_keys, grad_values), grad_query)

    zeros_kv = jnp.zeros((seq_len, heads_here, head_size), jnp.float32)
    (grad_keys, grad_values), grad_queries = lax.scan(
        one_block, (zeros_kv, zeros_kv), (query_blocks, grad_blocks, row_lse)
    )
    grad_queries = grad_queries.reshape(seq_len, heads_here, head_size)
    return jnp.stack([grad_queries, grad_keys, grad_values], axis=1).astype(jnp.bfloat16)


def per_device(
    hidden_in,
    seq_lengths,
    w_qkv,
    b_query,
    b_value,
    w_out,
    b_out,
    ln1_gain,
    ln1_bias,
    w_up,
    b_up,
    w_down,
    b_down,
    ln2_gain,
    ln2_bias,
    cotangent,
):
    group_count = lax.axis_size("seq")
    shard_count = lax.axis_size("shard")
    seq_count = hidden_in.shape[0]
    pos_count = hidden_in.shape[1]
    model_width = hidden_in.shape[2]
    tok_count = seq_count * pos_count
    full_len = pos_count * group_count
    group_width = model_width // group_count
    heads_here = group_width // DH
    block_rows = min(512, full_len)
    gathered = (
        lax.all_gather(w_qkv, "shard", axis=0, tiled=True),
        lax.all_gather(b_query, "shard", axis=0, tiled=True),
        lax.all_gather(b_value, "shard", axis=0, tiled=True),
        lax.all_gather(w_out, "shard", axis=0, tiled=True),
        lax.all_gather(b_out, "shard", axis=0, tiled=True),
        lax.all_gather(ln1_gain, "shard", axis=0, tiled=True),
        lax.all_gather(ln1_bias, "shard", axis=0, tiled=True),
        lax.all_gather(w_up, "shard", axis=0, tiled=True),
        lax.all_gather(b_up, "shard", axis=0, tiled=True),
        lax.all_gather(w_down, "shard", axis=0, tiled=True),
        lax.all_gather(b_down, "shard", axis=0, tiled=True),
        lax.all_gather(ln2_gain, "shard", axis=0, tiled=True),
        lax.all_gather(ln2_bias, "shard", axis=0, tiled=True),
    )
    (
        qkv_weight,
        query_bias,
        value_bias,
        out_weight,
        out_bias,
        gain_one,
        shift_one,
        up_weight,
        up_bias,
        down_weight,
        down_bias,
        gain_two,
        shift_two,
    ) = gathered
    gain_one = gain_one.astype(jnp.float32)
    gain_two = gain_two.astype(jnp.float32)
    tokens = hidden_in.reshape(tok_count, model_width)
    qkv_bias = jnp.concatenate([query_bias, jnp.zeros_like(query_bias), value_bias]).astype(
        jnp.float32
    )
    qkv_tok = (jnp.dot(tokens, qkv_weight, preferred_element_type=jnp.float32) + qkv_bias).astype(
        jnp.bfloat16
    )
    head_data = lax.all_to_all(
        qkv_tok.reshape(seq_count, pos_count, 3, group_count, group_width),
        "seq",
        split_axis=3,
        concat_axis=1,
        tiled=True,
    )
    head_data = head_data.reshape(seq_count, full_len, 3, heads_here, DH)
    attended_list = []
    lse_list = []
    for seq_pos in range(seq_count):
        out_seq, lse_seq = attend_forward(head_data[seq_pos], seq_lengths[seq_pos], block_rows)
        attended_list.append(out_seq)
        lse_list.append(lse_seq)
    attended_heads = (
        jnp.stack(attended_list).astype(jnp.bfloat16).reshape(seq_count, full_len, 1, group_width)
    )
    attended = lax.all_to_all(
        attended_heads, "seq", split_axis=1, concat_axis=2, tiled=True
    ).reshape(tok_count, model_width)
    projected = jnp.dot(attended, out_weight, preferred_element_type=jnp.float32) + out_bias.astype(
        jnp.float32
    )
    ln_one, normed_one, inv_one = norm_forward(
        tokens.astype(jnp.float32) + projected, gain_one, shift_one.astype(jnp.float32)
    )
    ln_low = ln_one.astype(jnp.bfloat16)
    pre_act = jnp.dot(ln_low, up_weight, preferred_element_type=jnp.float32) + up_bias.astype(
        jnp.float32
    )
    act_val, act_slope = gelu_parts(pre_act)
    act_low = act_val.astype(jnp.bfloat16)
    ffn_out = jnp.dot(act_low, down_weight, preferred_element_type=jnp.float32) + down_bias.astype(
        jnp.float32
    )
    result, normed_two, inv_two = norm_forward(
        ln_one + ffn_out, gain_two, shift_two.astype(jnp.float32)
    )
    output = result.astype(jnp.bfloat16).reshape(seq_count, pos_count, model_width)
    grad_y = cotangent.reshape(tok_count, model_width).astype(jnp.float32)
    grad_two, grad_gain_two, grad_shift_two = norm_backward(grad_y, normed_two, inv_two, gain_two)
    grad_ffn = grad_two.astype(jnp.bfloat16)
    grad_down_bias = jnp.sum(grad_ffn, axis=0, dtype=jnp.float32)
    grad_down_weight = dot_rows(act_low, grad_ffn)
    grad_pre = (dot_last(grad_ffn, down_weight) * act_slope).astype(jnp.bfloat16)
    grad_up_bias = jnp.sum(grad_pre, axis=0, dtype=jnp.float32)
    grad_up_weight = dot_rows(ln_low, grad_pre)
    grad_ln = dot_last(grad_pre, up_weight) + grad_two
    grad_one, grad_gain_one, grad_shift_one = norm_backward(grad_ln, normed_one, inv_one, gain_one)
    grad_proj = grad_one.astype(jnp.bfloat16)
    grad_out_bias = jnp.sum(grad_proj, axis=0, dtype=jnp.float32)
    grad_out_weight = dot_rows(attended, grad_proj)
    grad_att = dot_last(grad_proj, out_weight).astype(jnp.bfloat16)
    grad_heads = lax.all_to_all(
        grad_att.reshape(seq_count, pos_count, group_count, group_width),
        "seq",
        split_axis=2,
        concat_axis=1,
        tiled=True,
    )
    grad_heads = grad_heads.reshape(seq_count, full_len, heads_here, DH)
    grad_list = []
    for seq_pos in range(seq_count):
        grad_list.append(
            attend_backward(
                head_data[seq_pos],
                grad_heads[seq_pos],
                lse_list[seq_pos],
                seq_lengths[seq_pos],
                block_rows,
            )
        )
    grad_qkv_heads = jnp.stack(grad_list).reshape(seq_count, full_len, 3, 1, group_width)
    grad_qkv = lax.all_to_all(
        grad_qkv_heads, "seq", split_axis=1, concat_axis=3, tiled=True
    ).reshape(tok_count, 3 * model_width)
    grad_qkv_weight = dot_rows(tokens, grad_qkv)
    grad_query_bias = jnp.sum(grad_qkv[:, :model_width], axis=0, dtype=jnp.float32)
    grad_value_bias = jnp.sum(grad_qkv[:, 2 * model_width :], axis=0, dtype=jnp.float32)
    grad_input = (
        (dot_last(grad_qkv, qkv_weight) + grad_one)
        .astype(jnp.bfloat16)
        .reshape(seq_count, pos_count, model_width)
    )
    attn_list = (
        grad_qkv_weight,
        grad_query_bias,
        grad_value_bias,
        grad_out_weight,
        grad_out_bias,
        grad_gain_one,
        grad_shift_one,
    )
    every_grad = attn_list + (
        grad_up_weight,
        grad_up_bias,
        grad_down_weight,
        grad_down_bias,
        grad_gain_two,
        grad_shift_two,
    )
    every_grad = reorder_all(every_grad, shard_count, group_count)
    shares = (
        lax.psum_scatter(every_grad[0], ("seq", "shard"), scatter_dimension=0, tiled=True),
        lax.psum_scatter(every_grad[1], ("seq", "shard"), scatter_dimension=0, tiled=True),
        lax.psum_scatter(every_grad[2], ("seq", "shard"), scatter_dimension=0, tiled=True),
        lax.psum_scatter(every_grad[3], ("seq", "shard"), scatter_dimension=0, tiled=True),
        lax.psum_scatter(every_grad[4], ("seq", "shard"), scatter_dimension=0, tiled=True),
        lax.psum_scatter(every_grad[5], ("seq", "shard"), scatter_dimension=0, tiled=True),
        lax.psum_scatter(every_grad[6], ("seq", "shard"), scatter_dimension=0, tiled=True),
        lax.psum_scatter(every_grad[7], ("seq", "shard"), scatter_dimension=0, tiled=True),
        lax.psum_scatter(every_grad[8], ("seq", "shard"), scatter_dimension=0, tiled=True),
        lax.psum_scatter(every_grad[9], ("seq", "shard"), scatter_dimension=0, tiled=True),
        lax.psum_scatter(every_grad[10], ("seq", "shard"), scatter_dimension=0, tiled=True),
        lax.psum_scatter(every_grad[11], ("seq", "shard"), scatter_dimension=0, tiled=True),
        lax.psum_scatter(every_grad[12], ("seq", "shard"), scatter_dimension=0, tiled=True),
    )
    (
        share_qkv,
        share_qbias,
        share_vbias,
        share_outw,
        share_outb,
        share_gain_one,
        share_shift_one,
        share_upw,
        share_upb,
        share_downw,
        share_downb,
        share_gain_two,
        share_shift_two,
    ) = shares
    summed = (
        lax.all_gather(share_qkv.astype(jnp.bfloat16), "seq", axis=0, tiled=True).astype(
            share_qkv.dtype
        ),
        lax.all_gather(share_qbias.astype(jnp.bfloat16), "seq", axis=0, tiled=True).astype(
            share_qbias.dtype
        ),
        lax.all_gather(share_vbias.astype(jnp.bfloat16), "seq", axis=0, tiled=True).astype(
            share_vbias.dtype
        ),
        lax.all_gather(share_outw.astype(jnp.bfloat16), "seq", axis=0, tiled=True).astype(
            share_outw.dtype
        ),
        lax.all_gather(share_outb.astype(jnp.bfloat16), "seq", axis=0, tiled=True).astype(
            share_outb.dtype
        ),
        lax.all_gather(share_gain_one.astype(jnp.bfloat16), "seq", axis=0, tiled=True).astype(
            share_gain_one.dtype
        ),
        lax.all_gather(share_shift_one.astype(jnp.bfloat16), "seq", axis=0, tiled=True).astype(
            share_shift_one.dtype
        ),
        lax.all_gather(share_upw.astype(jnp.bfloat16), "seq", axis=0, tiled=True).astype(
            share_upw.dtype
        ),
        lax.all_gather(share_upb.astype(jnp.bfloat16), "seq", axis=0, tiled=True).astype(
            share_upb.dtype
        ),
        lax.all_gather(share_downw.astype(jnp.bfloat16), "seq", axis=0, tiled=True).astype(
            share_downw.dtype
        ),
        lax.all_gather(share_downb.astype(jnp.bfloat16), "seq", axis=0, tiled=True).astype(
            share_downb.dtype
        ),
        lax.all_gather(share_gain_two.astype(jnp.bfloat16), "seq", axis=0, tiled=True).astype(
            share_gain_two.dtype
        ),
        lax.all_gather(share_shift_two.astype(jnp.bfloat16), "seq", axis=0, tiled=True).astype(
            share_shift_two.dtype
        ),
    )
    return (
        output,
        grad_input,
        summed[0],
        summed[1],
        summed[2],
        summed[3],
        summed[4],
        summed[5],
        summed[6],
        summed[7],
        summed[8],
        summed[9],
        summed[10],
        summed[11],
        summed[12],
    )


def solution(mesh):
    in_specs = (
        P("shard", "seq", None),
        P("shard"),
        P("shard", None),
        P("shard"),
        P("shard"),
        P("shard", None),
        P("shard"),
        P("shard"),
        P("shard"),
        P("shard", None),
        P("shard"),
        P("shard", None),
        P("shard"),
        P("shard"),
        P("shard"),
        P("shard", "seq", None),
    )
    out_specs = (
        P("shard", "seq", None),
        P("shard", "seq", None),
        P("shard", None),
        P("shard"),
        P("shard"),
        P("shard", None),
        P("shard"),
        P("shard"),
        P("shard"),
        P("shard", None),
        P("shard"),
        P("shard", None),
        P("shard"),
        P("shard"),
        P("shard"),
    )
    return jax.shard_map(
        per_device, mesh=mesh, in_specs=in_specs, out_specs=out_specs, check_vma=False
    )
```

profile of v0, /device:TPU:0, one launch (start us, length us, event | category | flops | bytes accessed | tf_op | source)
XLA Modules:
  0.0 979.9 jit_solution(11414818758463418126)
XLA Ops:
  18.0 32.2 %all-reduce.27 = (bf16[768]{0:T(1024)(128)(2,1)S(1)}, bf16[768]{0:T(1024)(128)(2,1)S(1)}, bf16[768]{0:T(1024)(128)(2,1)}, bf16[768]{0:T(1024)(128)(2,1)}, bf16[7...) all-reduce(bf16[768]{0:T(1024)(128)(2,1)S(1)} %dynamic-update-slice, ...), channel_id=1, replica_groups=mesh['seq'=4,'shard'=8] {'shard'}, use_global_device_ids=true, to_apply=%add.1 | all-reduce | flops 6144 | bytes 24576
  54.5 8.5 add_convert_fusion
  63.1 12.8 %reshape.544 = bf16[2,512,3,4,192]{4,3,2,1,0:T(4,128)(2,1)} reshape(bf16[1024,2304]{1,0:T(8,128)(2,1)} %add_convert_fusion) | data formatting | bytes 9437184 | tf_op jit(solution)/shard_map/reshape | solution.py:211
  75.9 17.4 %copy.144 = bf16[2,512,3,4,192]{1,0,4,2,3:T(2,128)(2,1)} copy(bf16[2,512,3,4,192]{4,3,2,1,0:T(4,128)(2,1)} %reshape.544) | data formatting | bytes 9437184 | tf_op jit(solution)/shard_map/reshape | solution.py:211
  93.3 5.1 all-to-all-start
  99.6 52.5 %all-to-all-done = bf16[2,512,3,4,192]{1,0,4,2,3:T(2,128)(2,1)} async-done(((bf16[2,512,3,4,192]{1,0,4,2,3:T(2,128)(2,1)}), bf16[2,512,3,4,192]{1,0,4,2,3:T(2,128)(2,1)}, u32[]{:S(2)}, u32[]{:S(2)}) %all-to-all-start) | async-done | bytes 4718624 | tf_op jit(solution)/shard_map/all_to_all | solution.py:210
  152.1 10.6 %fusion.115 = (bf16[1,4,512,3,1,192]{2,0,5,3,1,4:T(2,128)(2,1)S(1)}, bf16[1,4,512,3,1,192]{2,0,5,3,1,4:T(2,128)(2,1)}) fusion(bf16[2,4,512,3,1,192]{2,0,5,3,1,4:T(2,128)(2,1)} %bitcast.3), kind=kLoop, calls=%fused_computation.175 | loop fusion | bytes 9437184 | tf_op jit(solution)/shard_map/slice | solution.py:221
  171.3 37.0 %while.56 = (s32[]{:T(128)}, bf16[4,512,3,64]{1,3,2,0:T(8,128)(2,1)S(1)}, f32[4,3,512]{2,1,0:T(4,128)S(1)}, bf16[4,512,3,64]{1,3,2,0:T(8,128)(2,1)S(1)}, bf16[20...) while((s32[]{:T(128)}, ...), condition=%wide.region_3.4_spmd.clone, body=%wide.region_0.3_spmd.clone.sunk | while | flops 843055616 | bytes 39979108 | solution.py:92
  208.3 7.7 copy.148
  216.0 5.9 squeeze.61
  227.4 39.2 %while.57 = (s32[]{:T(128)}, bf16[4,512,3,64]{1,3,2,0:T(8,128)(2,1)}, f32[4,3,512]{2,1,0:T(4,128)S(1)}, bf16[4,512,3,64]{1,3,2,0:T(8,128)(2,1)S(1)}, bf16[2048,3...) while((s32[]{:T(128)}, ...), condition=%wide.region_7.8_spmd.clone, body=%wide.region_4.7_spmd.clone.sunk | while | flops 843055616 | bytes 39975520 | solution.py:92
  276.9 6.1 copy.151
  287.7 12.7 %all-gather = bf16[8,1,384]{2,1,0:T(2,128)(2,1)S(1)} all-gather(bf16[1,1,384]{2,1,0:T(2,128)(2,1)S(1)} %reshape.506), channel_id=1, replica_groups=mesh['seq'=4,'shard'=8] {'shard'}, dimensions={0}, use_global_device_ids=true | all-gather | bytes 6912 | tf_op jit(solution)/shard_map/all_gather | solution.py:180
  301.8 10.6 %all-to-all-done.1 = bf16[2,2048,1,192]{3,0,2,1:T(2,128)(2,1)} async-done(((bf16[2,2048,1,192]{3,0,2,1:T(2,128)(2,1)}), bf16[2,2048,1,192]{3,0,2,1:T(2,128)(2,1)}, u32[]{:S(2)}, u32[]{:S(2)}) %all-to-all-start.1) | async-done | bytes 1572896 | tf_op jit(solution)/shard_map/all_to_all | solution.py:227
  312.4 6.1 copy.178
  326.1 12.1 %multiply_convert_fusion.2 = (bf16[1024,3072]{1,0:T(8,128)(2,1)}, f32[1024,3072]{1,0:T(8,128)}) fusion(f32[3072]{0:T(1024)S(1)} %bitcast.340, bf16[768,3072]{1,0:T(8,128)(2,1)} %all-gather.10.cloned.1.call-done, f32[1024,768]{1,0:T(8,128)S(1)} %get-tuple-element.615, f32[768]{0:T(1024)S(1)} %convert_element_type.210, f32[768]{0:T(1024)S(1)} %convert_element_type.209, ...), kind=kOutput, calls=%fused_computation.108 | convolution fusion | flops 4854644736 | bytes 26765312 | tf_op jit(solution)/shard_map/dot_general | solution.py:237
  338.2 8.8 fusion.119
  353.1 13.9 %convert_reduce_fusion = (f32[3072]{0:T(1024)}, bf16[1024,3072]{1,0:T(8,128)(2,1)S(1)}) fusion(f32[1024,3072]{1,0:T(8,128)} %get-tuple-element.617, f32[3072]{0:T(1024)S(1)} %bitcast.341, bf16[3072,768]{1,0:T(8,128)(2,1)S(1)} %copy-done.47, f32[1024,768]{1,0:T(8,128)S(1)} %get-tuple-element.590), kind=kOutput, calls=%fused_computation.107 | convolution fusion | flops 4873516032 | bytes 26763264 | tf_op jit(solution)/shard_map/dot_general | solution.py:20
  367.0 6.5 multiply_reduce_fusion.2
  378.7 7.9 fusion.110
  404.3 8.9 fusion.107
  418.0 5.0 all-to-all-done.2
  428.1 130.5 %while.58 = (s32[]{:T(128)}, f32[2048,3,64]{0,2,1:T(8,128)}, f32[2048,3,64]{0,2,1:T(8,128)}, bf16[4,512,3,64]{1,3,2,0:T(8,128)(2,1)}, bf16[4,512,3,64]{1,3,2,0:T...) while((s32[]{:T(128)}, f32[2048,3,64]{0,2,1:T(8,128)}, ...), condition=%wide.region_18.19_spmd.clone, body=%wide.region_16.18_spmd.clone.sunk | while | flops 2062516736 | bytes 204919504 | solution.py:136
  432.4 5.8 multiply_reduce_fusion.9
  438.2 5.0 multiply_convert_fusion.5
  443.2 5.5 fusion.209
  448.7 6.2 fusion.211
  464.0 5.8 multiply_reduce_fusion.9
  469.8 5.0 multiply_convert_fusion.5
  474.8 5.8 fusion.209
  480.6 6.2 fusion.211
  486.8 5.5 fusion.210
  496.5 5.8 multiply_reduce_fusion.9
  502.4 5.0 multiply_convert_fusion.5
  507.4 6.2 fusion.209
  513.6 6.7 fusion.211
  520.2 5.6 fusion.210
  530.0 5.8 multiply_reduce_fusion.9
  535.8 5.0 multiply_convert_fusion.5
  540.8 5.9 fusion.209
  546.7 6.4 fusion.211
  553.0 5.5 fusion.210
  562.0 122.0 %while.59 = (s32[]{:T(128)}, f32[2048,3,64]{0,2,1:T(8,128)S(1)}, f32[2048,3,64]{0,2,1:T(8,128)}, bf16[4,512,3,64]{1,3,2,0:T(8,128)(2,1)}, bf16[4,512,3,64]{1,3,2...) while((s32[]{:T(128)}, f32[2048,3,64]{0,2,1:T(8,128)S(1)}, ...), condition=%wide.region_21.22_spmd.clone, body=%wide.region_19.21_spmd.clone.sunk | while | flops 2062516736 | bytes 214356272 | solution.py:136
  581.4 5.6 fusion.224
  587.0 5.2 fusion.223
  610.8 5.7 fusion.224
  616.5 5.8 fusion.223
  641.3 6.0 fusion.224
  647.3 5.9 fusion.223
  662.5 5.0 multiply_convert_fusion.6
  671.8 6.4 fusion.224
  678.2 5.8 fusion.223
  701.5 16.1 %copy.159 = bf16[2,2048,3,1,192]{4,0,3,2,1:T(2,128)(2,1)} copy(bf16[2,2048,3,1,192]{1,4,3,2,0:T(8,128)(2,1)} %maximum_maximum_fusion) | data formatting | bytes 9437184 | tf_op jit(solution)/shard_map/stack | solution.py:282
  717.6 81.4 %all_to_all.60 = bf16[2,2048,3,1,192]{4,0,3,2,1:T(2,128)(2,1)} all-to-all(bf16[2,2048,3,1,192]{4,0,3,2,1:T(2,128)(2,1)} %copy.159), channel_id=1, replica_groups=mesh['seq'=4,'shard'=8] {'seq'}, dimensions={1} | all-to-all | bytes 9437184 | tf_op jit(solution)/shard_map/all_to_all | solution.py:283
  799.0 16.9 %copy.179 = bf16[2,4,512,3,1,192]{2,1,5,3,0,4:T(4,128)(2,1)} copy(bf16[2,4,512,3,1,192]{5,0,3,2,1,4:T(2,128)(2,1)} %bitcast.309) | data formatting | bytes 9437184 | tf_op jit(solution)/shard_map/all_to_all | solution.py:283
  815.9 9.4 copy.161
  841.8 9.0 all_gather.94
  854.4 40.1 %all-reduce.26 = (bf16[768]{0:T(1024)(128)(2,1)S(1)}, bf16[768]{0:T(1024)(128)(2,1)S(1)}, bf16[768]{0:T(1024)(128)(2,1)S(1)}, bf16[768]{0:T(1024)(128)(2,1)S(1)}...) all-reduce(f32[768]{0:T(1024)S(1)} %reshape.432, ...), channel_id=3, replica_groups=mesh['seq'=4,'shard'=8] {'seq','shard'}, use_global_device_ids=true, to_apply=%region_24.25.clone | all-reduce | flops 9216 | bytes 55296
  897.2 9.9 %all-reduce.28 = (bf16[96]{0:T(256)(128)(2,1)S(1)}, bf16[96]{0:T(256)(128)(2,1)S(1)}, bf16[96]{0:T(256)(128)(2,1)S(1)}, bf16[96]{0:T(256)(128)(2,1)S(1)}, bf16[9...) all-reduce(bf16[96]{0:T(256)(128)(2,1)S(1)} %dynamic-update-slice.8, ...), channel_id=1, replica_groups=mesh['seq'=4,'shard'=8] {'seq'}, use_global_device_ids=true, to_apply=%add.8 | all-reduce | flops 1152 | bytes 4608
  911.8 8.5 add_convert_fusion.1
  921.3 12.6 %all_gather.98 = bf16[96,3072]{1,0:T(8,128)(2,1)S(1)} all-gather(bf16[24,3072]{1,0:T(8,128)(2,1)S(1)} %convert_element_type.243), channel_id=1, replica_groups=mesh['seq'=4,'shard'=8] {'seq'}, dimensions={0}, use_global_device_ids=true | all-gather | bytes 737280 | tf_op jit(solution)/shard_map/all_gather | solution.py:364
  936.0 10.4 %all_gather.100 = bf16[384,768]{1,0:T(8,128)(2,1)S(1)} all-gather(bf16[96,768]{1,0:T(8,128)(2,1)S(1)} %convert_element_type.248), channel_id=1, replica_groups=mesh['seq'=4,'shard'=8] {'seq'}, dimensions={0}, use_global_device_ids=true | all-gather | bytes 737280 | tf_op jit(solution)/shard_map/all_gather | solution.py:370
  947.5 12.9 %reduce-scatter.5.cloned.1.call-done = f32[24,2304]{1,0:T(8,128)} async-done(((f32[768,2304]{1,0:T(8,128)}), f32[24,2304]{1,0:T(8,128)}) %reduce-scatter.5.cloned.1.call-update) | async-done | bytes 221200 | tf_op jit(solution)/shard_map/reduce_scatter | solution.py:313
  961.3 10.3 %all_gather.91 = bf16[96,2304]{1,0:T(8,128)(2,1)S(1)} all-gather(bf16[24,2304]{1,0:T(8,128)(2,1)S(1)} %convert_element_type.226), channel_id=1, replica_groups=mesh['seq'=4,'shard'=8] {'seq'}, dimensions={0}, use_global_device_ids=true | all-gather | bytes 552960 | tf_op jit(solution)/shard_map/all_gather | solution.py:343
  (411 shorter events, 312.8 us)
Async XLA Ops:
  7.2 47.3 %all-gather.6.cloned.1.call-start = ((), (), s32[]{:S(2)}) async-start(), calls=%async_computation.8 | async-start | bytes 3981312 | tf_op jit(solution)/shard_map/all_gather | solution.py:172
  7.9 313.8 %all-gather.8.cloned.1.call-start = ((), (), s32[]{:S(2)}) async-start(), calls=%async_computation.9 | async-start | bytes 1327104 | tf_op jit(solution)/shard_map/all_gather | solution.py:175
  8.7 317.4 %all-gather.10.cloned.1.call-start = ((), (), s32[]{:S(2)}) async-start(), calls=%async_computation.10 | async-start | bytes 5308416 | tf_op jit(solution)/shard_map/all_gather | solution.py:179
  93.3 5.7 copy-start.45
  93.3 58.8 %all-to-all-start = ((bf16[2,512,3,4,192]{1,0,4,2,3:T(2,128)(2,1)}), bf16[2,512,3,4,192]{1,0,4,2,3:T(2,128)(2,1)}, u32[]{:S(2)}, u32[]{:S(2)}) async-start(bf16[2,512,3,4,192]{1,0,4,2,3:T(2,128)(2,1)} %copy.144), calls=%async_computation | async-start | bytes 9437184 | tf_op jit(solution)/shard_map/all_to_all | solution.py:210
  98.4 239.8 %all-gather.12.cloned.1.call-start = ((), (), s32[]{:S(2)}) async-start(), calls=%async_computation.11 | async-start | bytes 5308416 | tf_op jit(solution)/shard_map/all_gather | solution.py:181
  208.3 7.7 copy-start.6
  208.3 7.7 copy-start.12
  208.3 7.7 copy-start.14
  208.3 7.7 copy-start.30
  266.5 10.3 %copy-start.4 = (bf16[2048,3,64]{0,2,1:T(8,128)(2,1)}, bf16[2048,3,64]{0,2,1:T(8,128)(2,1)S(1)}, u32[]{:S(2)}) copy-start(bf16[2048,3,64]{0,2,1:T(8,128)(2,1)S(1)} %get-tuple-element.977) | copy-start | bytes 2359300
  266.5 10.3 %copy-start.10 = (bf16[2048,3,64]{0,2,1:T(8,128)(2,1)}, bf16[2048,3,64]{0,2,1:T(8,128)(2,1)S(1)}, u32[]{:S(2)}) copy-start(bf16[2048,3,64]{0,2,1:T(8,128)(2,1)S(1)} %get-tuple-element.979) | copy-start | bytes 2359300
  266.5 10.3 %copy-start.13 = (bf16[4,512,3,64]{1,3,2,0:T(8,128)(2,1)}, bf16[4,512,3,64]{1,3,2,0:T(8,128)(2,1)S(1)}, u32[]{:S(2)}) copy-start(bf16[4,512,3,64]{1,3,2,0:T(8,128)(2,1)S(1)} %get-tuple-element.989) | copy-start | bytes 2359300
  266.5 10.3 %copy-start.31 = (f32[4,3,512]{2,1,0:T(4,128)}, f32[4,3,512]{2,1,0:T(4,128)S(1)}, u32[]{:S(2)}) copy-start(f32[4,3,512]{2,1,0:T(4,128)S(1)} %get-tuple-element.903) | copy-start | bytes 73732
  276.9 10.8 %copy-start.44 = (bf16[768]{0:T(1024)(128)(2,1)S(1)}, bf16[768]{0:T(1024)(128)(2,1)}, u32[]{:S(2)}) copy-start(bf16[768]{0:T(1024)(128)(2,1)} %get-tuple-element.574) | copy-start | bytes 4612
  276.9 10.8 %copy-start.43 = (bf16[768]{0:T(1024)(128)(2,1)S(1)}, bf16[768]{0:T(1024)(128)(2,1)}, u32[]{:S(2)}) copy-start(bf16[768]{0:T(1024)(128)(2,1)} %get-tuple-element.576) | copy-start | bytes 4612
  276.9 10.8 %copy-start.42 = (bf16[768]{0:T(1024)(128)(2,1)S(1)}, bf16[768]{0:T(1024)(128)(2,1)}, u32[]{:S(2)}) copy-start(bf16[768]{0:T(1024)(128)(2,1)} %get-tuple-element.575) | copy-start | bytes 4612
  276.9 10.8 %copy-start.46 = (bf16[384]{0:T(512)(128)(2,1)S(1)}, bf16[384]{0:T(512)(128)(2,1)}, u32[]{:S(2)}) copy-start(bf16[384]{0:T(512)(128)(2,1)} %param.34) | copy-start | bytes 2308
  276.9 23.5 %copy-start.41 = (bf16[768]{0:T(1024)(128)(2,1)S(1)}, bf16[768]{0:T(1024)(128)(2,1)}, u32[]{:S(2)}) copy-start(bf16[768]{0:T(1024)(128)(2,1)} %get-tuple-element.577) | copy-start | bytes 4612
  276.9 23.5 %copy-start.40 = (bf16[768]{0:T(1024)(128)(2,1)S(1)}, bf16[768]{0:T(1024)(128)(2,1)}, u32[]{:S(2)}) copy-start(bf16[768]{0:T(1024)(128)(2,1)} %get-tuple-element.579) | copy-start | bytes 4612
  283.0 17.5 %copy-start.15 = (bf16[2,512,768]{2,1,0:T(8,128)(2,1)S(1)}, bf16[2,512,768]{2,1,0:T(8,128)(2,1)}, u32[]{:S(2)}) copy-start(bf16[2,512,768]{2,1,0:T(8,128)(2,1)} %param.39) | copy-start | bytes 4718596
  283.0 18.8 %copy-start.39 = (bf16[768]{0:T(1024)(128)(2,1)S(1)}, bf16[768]{0:T(1024)(128)(2,1)}, u32[]{:S(2)}) copy-start(bf16[768]{0:T(1024)(128)(2,1)} %get-tuple-element.578) | copy-start | bytes 4612
  283.0 29.3 %all-to-all-start.1 = ((bf16[2,2048,1,192]{3,0,2,1:T(2,128)(2,1)}), bf16[2,2048,1,192]{3,0,2,1:T(2,128)(2,1)}, u32[]{:S(2)}, u32[]{:S(2)}) async-start(bf16[2,2048,1,192]{3,0,2,1:T(2,128)(2,1)} %copy.151), calls=%async_computation.1 | async-start | bytes 4194304 | tf_op jit(solution)/shard_map/all_to_all | solution.py:227
  287.6 553.3 %reduce-scatter.7.cloned.1.call-start = ((), (), s32[]{:S(2)}) async-start(), calls=%async_computation.13 | async-start | bytes 2433024 | tf_op jit(solution)/shard_map/reduce_scatter | solution.py:316
  350.2 16.8 %slice-start = ((s8[4718592]{0:T(1024)(128)(4,1)}), s8[4194304]{0:T(1024)(128)(4,1)S(1)}, s32[]{:S(2)}) async-start(s8[4718592]{0:T(1024)(128)(4,1)} %bitcast.342), calls=%async_computation.16 | async-start | bytes 8388608
  353.1 13.9 %copy-start.19 = (f32[1024,768]{1,0:T(8,128)}, f32[1024,768]{1,0:T(8,128)S(1)}, u32[]{:S(2)}) copy-start(f32[1024,768]{1,0:T(8,128)S(1)} %get-tuple-element.590) | copy-start | bytes 9437188
  353.1 13.9 %slice-start.1 = ((s8[4718592]{0:T(1024)(128)(4,1)}), s8[524288]{0:T(1024)(128)(4,1)S(1)}, s32[]{:S(2)}) async-start(s8[4718592]{0:T(1024)(128)(4,1)} %bitcast.342), calls=%async_computation.17 | async-start | bytes 1048576
  367.0 6.5 copy-start.18
  378.7 541.6 %reduce-scatter.9.cloned.1.call-start = ((), (), s32[]{:S(2)}) async-start(), calls=%async_computation.14 | async-start | bytes 9732096 | tf_op jit(solution)/shard_map/reduce_scatter | solution.py:320
  400.7 22.2 %all-to-all-start.2 = ((bf16[2,512,4,192]{1,0,3,2:T(2,128)(2,1)}), bf16[2,512,4,192]{1,0,3,2:T(2,128)(2,1)S(1)}, u32[]{:S(2)}, u32[]{:S(2)}) async-start(bf16[2,512,4,192]{1,0,3,2:T(2,128)(2,1)} %reshape.426), calls=%async_computation.2 | async-start | bytes 3145728 | tf_op jit(solution)/shard_map/all_to_all | solution.py:263
  404.3 530.7 %reduce-scatter.11.cloned.1.call-start = ((), (), s32[]{:S(2)}) async-start(), calls=%async_computation.15 | async-start | bytes 9732096 | tf_op jit(solution)/shard_map/reduce_scatter | solution.py:322
  417.9 542.4 %reduce-scatter.5.cloned.1.call-start = ((), (), s32[]{:S(2)}) async-start(), calls=%async_computation.12 | async-start | bytes 7299072 | tf_op jit(solution)/shard_map/reduce_scatter | solution.py:313
  423.0 5.1 copy-start.7
  428.1 134.0 %copy-start.5 = (bf16[2048,3,64]{0,2,1:T(8,128)(2,1)S(1)}, bf16[2048,3,64]{0,2,1:T(8,128)(2,1)}, u32[]{:S(2)}) copy-start(bf16[2048,3,64]{0,2,1:T(8,128)(2,1)} %copy-done.4) | copy-start | bytes 2359300
  428.1 134.0 %copy-start.8 = (f32[2048,3,64]{0,2,1:T(8,128)S(1)}, f32[2048,3,64]{0,2,1:T(8,128)}, u32[]{:S(2)}) copy-start(f32[2048,3,64]{0,2,1:T(8,128)} %custom-call.2) | copy-start | bytes 4718596
  431.0 7.3 copy-start
  443.2 11.7 %copy-start.1 = (f32[3,512,2048]{2,1,0:T(8,128)S(1)}, f32[3,512,2048]{2,1,0:T(8,128)}, u32[]{:S(2)}) copy-start(f32[3,512,2048]{2,1,0:T(8,128)} %copy-done) | copy-start | bytes 37748740 | tf_op jit(solution)/shard_map/while
  462.6 7.2 copy-start
  474.8 12.0 %copy-start.1 = (f32[3,512,2048]{2,1,0:T(8,128)S(1)}, f32[3,512,2048]{2,1,0:T(8,128)}, u32[]{:S(2)}) copy-start(f32[3,512,2048]{2,1,0:T(8,128)} %copy-done) | copy-start | bytes 37748740 | tf_op jit(solution)/shard_map/while
  495.1 7.3 copy-start
  507.4 12.9 %copy-start.1 = (f32[3,512,2048]{2,1,0:T(8,128)S(1)}, f32[3,512,2048]{2,1,0:T(8,128)}, u32[]{:S(2)}) copy-start(f32[3,512,2048]{2,1,0:T(8,128)} %copy-done) | copy-start | bytes 37748740 | tf_op jit(solution)/shard_map/while
  528.6 7.2 copy-start
  540.8 12.2 %copy-start.1 = (f32[3,512,2048]{2,1,0:T(8,128)S(1)}, f32[3,512,2048]{2,1,0:T(8,128)}, u32[]{:S(2)}) copy-start(f32[3,512,2048]{2,1,0:T(8,128)} %copy-done) | copy-start | bytes 37748740 | tf_op jit(solution)/shard_map/while
  562.2 4.3 copy-start.11
  565.0 6.4 copy-start.2
  571.4 9.9 %copy-start.23 = (bf16[4,512,3,64]{1,3,2,0:T(8,128)(2,1)S(1)}, bf16[4,512,3,64]{1,3,2,0:T(8,128)(2,1)}, u32[]{:S(2)}) copy-start(bf16[4,512,3,64]{1,3,2,0:T(8,128)(2,1)} %get-tuple-element.912) | copy-start | bytes 2359300 | tf_op jit(solution)/shard_map/while
  576.4 10.5 %copy-start.3 = (f32[3,512,2048]{2,1,0:T(8,128)S(1)}, f32[3,512,2048]{2,1,0:T(8,128)}, u32[]{:S(2)}) copy-start(f32[3,512,2048]{2,1,0:T(8,128)} %copy-done.2) | copy-start | bytes 37748740 | tf_op jit(solution)/shard_map/while
  586.9 5.2 copy-start.24
  592.1 4.3 copy-start.11
  595.0 6.4 copy-start.2
  601.4 9.4 copy-start.23
  606.4 10.1 %copy-start.3 = (f32[3,512,2048]{2,1,0:T(8,128)S(1)}, f32[3,512,2048]{2,1,0:T(8,128)}, u32[]{:S(2)}) copy-start(f32[3,512,2048]{2,1,0:T(8,128)} %copy-done.2) | copy-start | bytes 37748740 | tf_op jit(solution)/shard_map/while
  616.5 5.8 copy-start.24
  625.2 6.4 copy-start.2
  631.6 9.7 copy-start.23
  636.6 10.7 %copy-start.3 = (f32[3,512,2048]{2,1,0:T(8,128)S(1)}, f32[3,512,2048]{2,1,0:T(8,128)}, u32[]{:S(2)}) copy-start(f32[3,512,2048]{2,1,0:T(8,128)} %copy-done.2) | copy-start | bytes 37748740 | tf_op jit(solution)/shard_map/while
  647.3 5.9 copy-start.24
  653.1 4.3 copy-start.11
  656.0 6.4 copy-start.2
  662.4 9.4 copy-start.23
  667.4 10.8 %copy-start.3 = (f32[3,512,2048]{2,1,0:T(8,128)S(1)}, f32[3,512,2048]{2,1,0:T(8,128)}, u32[]{:S(2)}) copy-start(f32[3,512,2048]{2,1,0:T(8,128)} %copy-done.2) | copy-start | bytes 37748740 | tf_op jit(solution)/shard_map/while
  678.2 5.8 copy-start.24
  684.0 5.5 copy-start.9
  837.0 74.7 %copy-start.28 = (f32[1024,768]{1,0:T(8,128)S(1)}, f32[1024,768]{1,0:T(8,128)}, u32[]{:S(2)}) copy-start(f32[1024,768]{1,0:T(8,128)} %copy-done.26) | copy-start | bytes 9437188
  (20 other events, 54.4 us)
Sparse Core Ops, SparseCore 0:
  9.7 44.8 all-gather.5
  56.2 21.5 all-gather.7
  79.4 51.4 all-gather.9
  132.4 50.5 all-gather.11
  378.8 97.0 reduce-scatter.6
  482.7 134.6 reduce-scatter.8
  623.2 153.8 reduce-scatter.10
  837.2 123.1 reduce-scatter.4
where the time goes:
time: 990 us; the launch traced here: 980 us
  matrix products  337 us (34%)
  blocking collectives  219 us (22%)
  local copies, waits for them, and re-layouts  197 us (20%)
  other arithmetic  107 us (11%)
  waiting for transfers between devices  87.7 us (9%)
  between operations  17.5 us (2%)
  starting transfers between devices  13.8 us (1%)
    unnamed x3, blocking collectives  82.3 us
    all_to_all x1, blocking collectives, per_device(): lax.all_to_all(grad_qkv_heads, 'seq', split_axis=1, concat_axis=3, tiled=...  81.4 us
    all_to_all x1, waiting for transfers between devices, per_device(): lax.all_to_all(qkv_tok.reshape(seq_count, pos_count, 3, group_count, grou...  52.5 us
    dot_general x8, matrix products, one_block(): jnp.einsum('hbk,khd->bhd', grad_scores, keys_all, preferred_element_type=...  48.9 us
    dot_general x8, matrix products, one_block(): jnp.einsum('hbk,bhd->khd', attn_prob.astype(jnp.bfloat16), grad_blk, pref...  44.2 us
    dot_general x8, matrix products, one_block(): jnp.einsum('bhd,khd->hbk', grad_blk, values_all, preferred_element_type=j...  42.9 us
    dot_general x8, matrix products, one_block(): jnp.einsum('hbk,bhd->khd', grad_scores, query_blk, preferred_element_type...  41.9 us
    convert_element_type x8, other arithmetic, one_block(): grad_scores = (attn_prob * (grad_prob - row_dot)).astype(jnp.bfloat16)  39.8 us
  transfers between devices with their start and end apart: 11, of which 5 were waited for; matrix products, arithmetic and copies ran while one was open for 61% of the time, Pallas kernels for 0%

commit v1 on v0

--- a/solution.py
+++ b/solution.py
@@ -224,9 +224,16 @@
     attended_heads = (
         jnp.stack(attended_list).astype(jnp.bfloat16).reshape(seq_count, full_len, 1, group_width)
     )
-    attended = lax.all_to_all(
-        attended_heads, "seq", split_axis=1, concat_axis=2, tiled=True
-    ).reshape(tok_count, model_width)
+    list_shards = lambda buf, lane_axis: jnp.concatenate(
+        lax.all_to_all(
+            jnp.stack(jnp.split(buf, lax.axis_size(lane_axis), 1), axis=0),
+            axis_name=lane_axis,
+            split_axis=0,
+            concat_axis=0,
+        ),
+        2,
+    )
+    attended = list_shards(attended_heads, "seq").reshape(tok_count, model_width)
     projected = jnp.dot(attended, out_weight, preferred_element_type=jnp.float32) + out_bias.astype(
         jnp.float32
     )

time: 990 us -> 971 us (0.981)
  matrix products: 337 us -> 326 us
    unnamed x144 -> x133, local copies, waits for them, and re-layouts: 25.6 us -> 25.7 us
  transfers between devices with their start and end apart: 11 -> 11, of which waited for: 5 -> 5; matrix products, arithmetic and copies ran while one was open for 61% -> 60% of each run, Pallas kernels for 0% -> 0%
where the time goes in v1:
time: 971 us; the launch traced here: 961 us
  matrix products  326 us (34%)
  blocking collectives  224 us (23%)
  local copies, waits for them, and re-layouts  190 us (20%)
  other arithmetic  109 us (11%)
  waiting for transfers between devices  80.1 us (8%)
  between operations  17.5 us (2%)
  starting transfers between devices  14.5 us (1%)
    all_to_all x1, blocking collectives, per_device(): lax.all_to_all(grad_qkv_heads, 'seq', split_axis=1, concat_axis=3, tiled=...  87 us
    unnamed x3, blocking collectives  82.3 us
    all_to_all x1, waiting for transfers between devices, per_device(): lax.all_to_all(qkv_tok.reshape(seq_count, pos_count, 3, group_count, grou...  52.5 us
    dot_general x8, matrix products, one_block(): jnp.einsum('hbk,khd->bhd', grad_scores, keys_all, preferred_element_type=...  51.3 us
    dot_general x8, matrix products, one_block(): jnp.einsum('hbk,bhd->khd', attn_prob.astype(jnp.bfloat16), grad_blk, pref...  41.2 us
    dot_general x8, matrix products, one_block(): jnp.einsum('hbk,bhd->khd', grad_scores, query_blk, preferred_element_type...  41 us
    convert_element_type x8, other arithmetic, one_block(): grad_scores = (attn_prob * (grad_prob - row_dot)).astype(jnp.bfloat16)  39.6 us
    dot_general x8, matrix products, one_block(): jnp.einsum('bhd,khd->hbk', grad_blk, values_all, preferred_element_type=j...  34.7 us
  transfers between devices with their start and end apart: 11, of which 5 were waited for; matrix products, arithmetic and copies ran while one was open for 60% of the time, Pallas kernels for 0%

profile of v1, /device:TPU:0, one launch (start us, length us, event | category | flops | bytes accessed | tf_op | source)
XLA Modules:
  0.0 961.1 jit_solution(6716818135580783000)
XLA Ops:
  18.0 32.2 %all-reduce.27 = (bf16[768]{0:T(1024)(128)(2,1)S(1)}, bf16[768]{0:T(1024)(128)(2,1)S(1)}, bf16[768]{0:T(1024)(128)(2,1)}, bf16[768]{0:T(1024)(128)(2,1)}, bf16[7...) all-reduce(bf16[768]{0:T(1024)(128)(2,1)S(1)} %dynamic-update-slice, ...), channel_id=1, replica_groups=mesh['seq'=4,'shard'=8] {'shard'}, use_global_device_ids=true, to_apply=%add.1 | all-reduce | flops 6144 | bytes 24576
  54.5 8.5 add_convert_fusion
  63.0 12.8 %reshape.543 = bf16[2,512,3,4,192]{4,3,2,1,0:T(4,128)(2,1)} reshape(bf16[1024,2304]{1,0:T(8,128)(2,1)} %add_convert_fusion) | data formatting | bytes 9437184 | tf_op jit(solution)/shard_map/reshape | solution.py:211
  75.9 17.4 %copy.155 = bf16[2,512,3,4,192]{1,0,4,2,3:T(2,128)(2,1)} copy(bf16[2,512,3,4,192]{4,3,2,1,0:T(4,128)(2,1)} %reshape.543) | data formatting | bytes 9437184 | tf_op jit(solution)/shard_map/reshape | solution.py:211
  93.3 5.1 all-to-all-start
  99.6 52.5 %all-to-all-done = bf16[2,512,3,4,192]{1,0,4,2,3:T(2,128)(2,1)} async-done(((bf16[2,512,3,4,192]{1,0,4,2,3:T(2,128)(2,1)}), bf16[2,512,3,4,192]{1,0,4,2,3:T(2,128)(2,1)}, u32[]{:S(2)}, u32[]{:S(2)}) %all-to-all-start) | async-done | bytes 4718624 | tf_op jit(solution)/shard_map/all_to_all | solution.py:210
  152.0 10.6 %fusion.115 = (bf16[1,4,512,3,1,192]{2,0,5,3,1,4:T(2,128)(2,1)S(1)}, bf16[1,4,512,3,1,192]{2,0,5,3,1,4:T(2,128)(2,1)}) fusion(bf16[2,4,512,3,1,192]{2,0,5,3,1,4:T(2,128)(2,1)} %bitcast.3), kind=kLoop, calls=%fused_computation.181 | loop fusion | bytes 9437184 | tf_op jit(solution)/shard_map/slice | solution.py:221
  171.2 37.0 %while.57 = (s32[]{:T(128)}, bf16[4,512,3,64]{1,3,2,0:T(8,128)(2,1)S(1)}, f32[4,3,512]{2,1,0:T(4,128)S(1)}, bf16[4,512,3,64]{1,3,2,0:T(8,128)(2,1)S(1)}, bf16[20...) while((s32[]{:T(128)}, ...), condition=%wide.region_7.8_spmd.clone, body=%wide.region_4.7_spmd.clone.sunk | while | flops 843055616 | bytes 39979108 | solution.py:92
  208.3 7.6 copy.156
  216.0 5.9 squeeze.57
  227.3 39.2 %while.56 = (s32[]{:T(128)}, bf16[4,512,3,64]{1,3,2,0:T(8,128)(2,1)}, f32[4,3,512]{2,1,0:T(4,128)S(1)}, bf16[4,512,3,64]{1,3,2,0:T(8,128)(2,1)S(1)}, bf16[2048,3...) while((s32[]{:T(128)}, ...), condition=%wide.region_3.4_spmd.clone, body=%wide.region_0.3_spmd.clone.sunk | while | flops 843055616 | bytes 39975520 | solution.py:92
  283.4 12.7 %all-gather = bf16[8,1,384]{2,1,0:T(2,128)(2,1)S(1)} all-gather(bf16[1,1,384]{2,1,0:T(2,128)(2,1)S(1)} %reshape.505), channel_id=1, replica_groups=mesh['seq'=4,'shard'=8] {'shard'}, dimensions={0}, use_global_device_ids=true | all-gather | bytes 6912 | tf_op jit(solution)/shard_map/all_gather | solution.py:180
  313.1 12.6 %multiply_convert_fusion.2 = (bf16[1024,3072]{1,0:T(8,128)(2,1)}, f32[1024,3072]{1,0:T(8,128)}) fusion(f32[3072]{0:T(1024)S(1)} %bitcast.349, bf16[768,3072]{1,0:T(8,128)(2,1)} %all-gather.10.cloned.1.call-done, f32[1024,768]{1,0:T(8,128)} %copy-done.9, f32[768]{0:T(1024)S(1)} %convert_element_type.210, f32[768]{0:T(1024)S(1)} %convert_element_type.209, ...), kind=kOutput, calls=%fused_computation.108 | convolution fusion | flops 4854644736 | bytes 26765312 | tf_op jit(solution)/shard_map/dot_general | solution.py:244
  325.6 9.3 fusion.119
  341.0 13.7 %convert_reduce_fusion = (f32[3072]{0:T(1024)}, bf16[1024,3072]{1,0:T(8,128)(2,1)S(1)}) fusion(f32[1024,3072]{1,0:T(8,128)} %get-tuple-element.620, f32[3072]{0:T(1024)S(1)} %bitcast.350, bf16[3072,768]{1,0:T(8,128)(2,1)S(1)} %copy-done.38, f32[1024,768]{1,0:T(8,128)S(1)} %get-tuple-element.590), kind=kOutput, calls=%fused_computation.107 | convolution fusion | flops 4873516032 | bytes 26763264 | tf_op jit(solution)/shard_map/dot_general | solution.py:20
  354.8 6.5 multiply_reduce_fusion.2
  366.4 8.9 fusion.110
  395.4 8.5 fusion.107
  408.6 5.5 all-to-all-done.2
  414.1 5.6 fusion.116
  420.9 113.5 %while.58 = (s32[]{:T(128)}, f32[2048,3,64]{0,2,1:T(8,128)}, f32[2048,3,64]{0,2,1:T(8,128)}, bf16[4,512,3,64]{1,3,2,0:T(8,128)(2,1)}, bf16[4,512,3,64]{1,3,2,0:T...) while((s32[]{:T(128)}, f32[2048,3,64]{0,2,1:T(8,128)}, ...), condition=%wide.region_18.19_spmd.clone, body=%wide.region_16.18_spmd.clone.sunk | while | flops 2062516736 | bytes 204921552 | solution.py:136
  427.3 4.9 multiply_convert_fusion.5
  432.2 5.3 fusion.209
  437.5 6.2 fusion.211
  454.1 4.9 multiply_convert_fusion.5
  459.0 5.8 fusion.209
  464.8 6.2 fusion.211
  471.0 5.2 fusion.210
  482.9 4.9 multiply_convert_fusion.5
  487.8 6.1 fusion.209
  493.9 6.6 fusion.211
  500.5 5.2 fusion.210
  517.2 5.7 fusion.209
  522.9 6.2 fusion.211
  529.2 5.2 fusion.210
  538.0 122.5 %while.59 = (s32[]{:T(128)}, f32[2048,3,64]{0,2,1:T(8,128)S(1)}, f32[2048,3,64]{0,2,1:T(8,128)}, bf16[4,512,3,64]{1,3,2,0:T(8,128)(2,1)}, bf16[4,512,3,64]{1,3,2...) while((s32[]{:T(128)}, f32[2048,3,64]{0,2,1:T(8,128)S(1)}, ...), condition=%wide.region_21.22_spmd.clone, body=%wide.region_19.21_spmd.clone.sunk | while | flops 2062516736 | bytes 204919504 | solution.py:136
  542.4 4.9 multiply_reduce_fusion.10
  547.4 5.0 multiply_convert_fusion.6
  556.7 6.5 fusion.224
  563.2 4.9 fusion.223
  572.3 4.9 multiply_reduce_fusion.10
  577.3 5.0 multiply_convert_fusion.6
  586.7 6.2 fusion.224
  593.0 5.5 fusion.223
  602.7 4.9 multiply_reduce_fusion.10
  607.7 5.0 multiply_convert_fusion.6
  617.2 6.7 fusion.224
  623.9 5.6 fusion.223
  633.7 5.0 multiply_reduce_fusion.10
  638.7 5.0 multiply_convert_fusion.6
  648.4 6.6 fusion.224
  655.0 5.5 fusion.223
  678.3 16.1 %copy.171 = bf16[2,2048,3,1,192]{4,0,3,2,1:T(2,128)(2,1)} copy(bf16[2,2048,3,1,192]{1,4,3,2,0:T(8,128)(2,1)} %maximum_maximum_fusion) | data formatting | bytes 9437184 | tf_op jit(solution)/shard_map/stack | solution.py:289
  694.4 87.0 %all_to_all.50 = bf16[2,2048,3,1,192]{4,0,3,2,1:T(2,128)(2,1)} all-to-all(bf16[2,2048,3,1,192]{4,0,3,2,1:T(2,128)(2,1)} %copy.171), channel_id=1, replica_groups=mesh['seq'=4,'shard'=8] {'seq'}, dimensions={1} | all-to-all | bytes 9437184 | tf_op jit(solution)/shard_map/all_to_all | solution.py:290
  781.4 16.9 %copy.190 = bf16[2,4,512,3,1,192]{2,1,5,3,0,4:T(4,128)(2,1)} copy(bf16[2,4,512,3,1,192]{5,0,3,2,1,4:T(2,128)(2,1)} %bitcast.319) | data formatting | bytes 9437184 | tf_op jit(solution)/shard_map/all_to_all | solution.py:290
  798.4 9.4 copy.173
  824.3 8.8 all_gather.94
  836.6 40.2 %all-reduce.26 = (bf16[768]{0:T(1024)(128)(2,1)S(1)}, bf16[768]{0:T(1024)(128)(2,1)S(1)}, bf16[768]{0:T(1024)(128)(2,1)S(1)}, bf16[768]{0:T(1024)(128)(2,1)S(1)}...) all-reduce(f32[768]{0:T(1024)S(1)} %reshape.431, ...), channel_id=3, replica_groups=mesh['seq'=4,'shard'=8] {'seq','shard'}, use_global_device_ids=true, to_apply=%region_24.25.clone | all-reduce | flops 9216 | bytes 55296
  879.5 9.9 %all-reduce.28 = (bf16[96]{0:T(256)(128)(2,1)S(1)}, bf16[96]{0:T(256)(128)(2,1)S(1)}, bf16[96]{0:T(256)(128)(2,1)S(1)}, bf16[96]{0:T(256)(128)(2,1)S(1)}, bf16[9...) all-reduce(bf16[96]{0:T(256)(128)(2,1)S(1)} %dynamic-update-slice.8, ...), channel_id=1, replica_groups=mesh['seq'=4,'shard'=8] {'seq'}, use_global_device_ids=true, to_apply=%add.8 | all-reduce | flops 1152 | bytes 4608
  894.0 8.5 add_convert_fusion.1
  903.6 12.5 %all_gather.98 = bf16[96,3072]{1,0:T(8,128)(2,1)S(1)} all-gather(bf16[24,3072]{1,0:T(8,128)(2,1)S(1)} %convert_element_type.243), channel_id=1, replica_groups=mesh['seq'=4,'shard'=8] {'seq'}, dimensions={0}, use_global_device_ids=true | all-gather | bytes 737280 | tf_op jit(solution)/shard_map/all_gather | solution.py:371
  918.2 10.4 %all_gather.100 = bf16[384,768]{1,0:T(8,128)(2,1)S(1)} all-gather(bf16[96,768]{1,0:T(8,128)(2,1)S(1)} %convert_element_type.248), channel_id=1, replica_groups=mesh['seq'=4,'shard'=8] {'seq'}, dimensions={0}, use_global_device_ids=true | all-gather | bytes 737280 | tf_op jit(solution)/shard_map/all_gather | solution.py:377
  929.7 11.9 %reduce-scatter.5.cloned.1.call-done = f32[24,2304]{1,0:T(8,128)} async-done(((f32[768,2304]{1,0:T(8,128)}), f32[24,2304]{1,0:T(8,128)}) %reduce-scatter.5.cloned.1.call-update) | async-done | bytes 221200 | tf_op jit(solution)/shard_map/reduce_scatter | solution.py:320
  942.5 10.3 %all_gather.91 = bf16[96,2304]{1,0:T(8,128)(2,1)S(1)} all-gather(bf16[24,2304]{1,0:T(8,128)(2,1)S(1)} %convert_element_type.226), channel_id=1, replica_groups=mesh['seq'=4,'shard'=8] {'seq'}, dimensions={0}, use_global_device_ids=true | all-gather | bytes 552960 | tf_op jit(solution)/shard_map/all_gather | solution.py:350
  (377 shorter events, 298.8 us)
Async XLA Ops:
  7.2 47.3 %all-gather.6.cloned.1.call-start = ((), (), s32[]{:S(2)}) async-start(), calls=%async_computation.8 | async-start | bytes 3981312 | tf_op jit(solution)/shard_map/all_gather | solution.py:172
  7.9 299.0 %all-gather.8.cloned.1.call-start = ((), (), s32[]{:S(2)}) async-start(), calls=%async_computation.9 | async-start | bytes 1327104 | tf_op jit(solution)/shard_map/all_gather | solution.py:175
  8.7 304.4 %all-gather.10.cloned.1.call-start = ((), (), s32[]{:S(2)}) async-start(), calls=%async_computation.10 | async-start | bytes 5308416 | tf_op jit(solution)/shard_map/all_gather | solution.py:179
  93.3 5.7 copy-start.36
  93.3 58.8 %all-to-all-start = ((bf16[2,512,3,4,192]{1,0,4,2,3:T(2,128)(2,1)}), bf16[2,512,3,4,192]{1,0,4,2,3:T(2,128)(2,1)}, u32[]{:S(2)}, u32[]{:S(2)}) async-start(bf16[2,512,3,4,192]{1,0,4,2,3:T(2,128)(2,1)} %copy.155), calls=%async_computation | async-start | bytes 9437184 | tf_op jit(solution)/shard_map/all_to_all | solution.py:210
  98.4 227.2 %all-gather.12.cloned.1.call-start = ((), (), s32[]{:S(2)}) async-start(), calls=%async_computation.11 | async-start | bytes 5308416 | tf_op jit(solution)/shard_map/all_gather | solution.py:181
  208.2 7.7 copy-start.4
  208.3 7.7 copy-start.7
  208.3 7.7 copy-start.11
  208.3 7.7 copy-start.22
  277.3 5.9 copy-start.35
  277.3 6.0 copy-start.34
  277.4 6.0 copy-start.33
  277.4 6.0 copy-start.37
  277.4 18.7 %copy-start.32 = (bf16[768]{0:T(1024)(128)(2,1)S(1)}, bf16[768]{0:T(1024)(128)(2,1)}, u32[]{:S(2)}) copy-start(bf16[768]{0:T(1024)(128)(2,1)} %get-tuple-element.577) | copy-start | bytes 4612
  277.4 18.7 %copy-start.31 = (bf16[768]{0:T(1024)(128)(2,1)S(1)}, bf16[768]{0:T(1024)(128)(2,1)}, u32[]{:S(2)}) copy-start(bf16[768]{0:T(1024)(128)(2,1)} %get-tuple-element.579) | copy-start | bytes 4612
  278.7 20.1 %copy-start.30 = (bf16[768]{0:T(1024)(128)(2,1)S(1)}, bf16[768]{0:T(1024)(128)(2,1)}, u32[]{:S(2)}) copy-start(bf16[768]{0:T(1024)(128)(2,1)} %get-tuple-element.578) | copy-start | bytes 4612
  278.7 23.6 %all-to-all-start.1 = ((bf16[4,2,512,1,192]{2,4,1,3,0:T(8,128)(2,1)}), bf16[4,2,512,1,192]{2,4,1,3,0:T(8,128)(2,1)}, u32[]{:S(2)}, u32[]{:S(2)}) async-start(bf16[4,2,512,1,192]{2,4,1,3,0:T(8,128)(2,1)} %pad_maximum_fusion), calls=%async_computation.1 | async-start | bytes 3145728 | tf_op jit(solution)/shard_map/all_to_all | solution.py:228
  283.2 540.1 %reduce-scatter.7.cloned.1.call-start = ((), (), s32[]{:S(2)}) async-start(), calls=%async_computation.13 | async-start | bytes 2433024 | tf_op jit(solution)/shard_map/reduce_scatter | solution.py:323
  310.9 1.6 copy-start.9
  334.9 1.4 copy-start.12
  338.1 2.9 copy-start.38
  338.1 16.6 %slice-start = ((s8[4718592]{0:T(1024)(128)(4,1)}), s8[4194304]{0:T(1024)(128)(4,1)S(1)}, s32[]{:S(2)}) async-start(s8[4718592]{0:T(1024)(128)(4,1)} %bitcast.351), calls=%async_computation.16 | async-start | bytes 8388608
  341.0 13.7 %copy-start.15 = (f32[1024,768]{1,0:T(8,128)}, f32[1024,768]{1,0:T(8,128)S(1)}, u32[]{:S(2)}) copy-start(f32[1024,768]{1,0:T(8,128)S(1)} %get-tuple-element.590) | copy-start | bytes 9437188
  341.0 13.7 %copy-start.10 = (f32[1024,768]{1,0:T(8,128)S(1)}, f32[1024,768]{1,0:T(8,128)}, u32[]{:S(2)}) copy-start(f32[1024,768]{1,0:T(8,128)} %copy-done.9) | copy-start | bytes 9437188
  341.0 13.7 %slice-start.1 = ((s8[4718592]{0:T(1024)(128)(4,1)}), s8[524288]{0:T(1024)(128)(4,1)S(1)}, s32[]{:S(2)}) async-start(s8[4718592]{0:T(1024)(128)(4,1)} %bitcast.351), calls=%async_computation.17 | async-start | bytes 1048576
  354.7 6.6 copy-start.14
  361.3 1.7 copy-start.21
  363.0 1.7 copy-start.19
  366.3 536.2 %reduce-scatter.9.cloned.1.call-start = ((), (), s32[]{:S(2)}) async-start(), calls=%async_computation.14 | async-start | bytes 9732096 | tf_op jit(solution)/shard_map/reduce_scatter | solution.py:327
  391.0 23.1 %all-to-all-start.2 = ((bf16[2,512,4,192]{1,0,3,2:T(2,128)(2,1)}), bf16[2,512,4,192]{1,0,3,2:T(2,128)(2,1)}, u32[]{:S(2)}, u32[]{:S(2)}) async-start(bf16[2,512,4,192]{1,0,3,2:T(2,128)(2,1)} %reshape.425), calls=%async_computation.2 | async-start | bytes 3145728 | tf_op jit(solution)/shard_map/all_to_all | solution.py:270
  395.3 521.8 %reduce-scatter.11.cloned.1.call-start = ((), (), s32[]{:S(2)}) async-start(), calls=%async_computation.15 | async-start | bytes 9732096 | tf_op jit(solution)/shard_map/reduce_scatter | solution.py:329
  408.5 533.0 %reduce-scatter.5.cloned.1.call-start = ((), (), s32[]{:S(2)}) async-start(), calls=%async_computation.12 | async-start | bytes 7299072 | tf_op jit(solution)/shard_map/reduce_scatter | solution.py:320
  422.7 4.5 copy-start
  432.2 11.6 %copy-start.1 = (f32[3,512,2048]{2,1,0:T(8,128)S(1)}, f32[3,512,2048]{2,1,0:T(8,128)}, u32[]{:S(2)}) copy-start(f32[3,512,2048]{2,1,0:T(8,128)} %copy-done) | copy-start | bytes 37748740 | tf_op jit(solution)/shard_map/while
  449.6 4.5 copy-start
  459.0 12.0 %copy-start.1 = (f32[3,512,2048]{2,1,0:T(8,128)S(1)}, f32[3,512,2048]{2,1,0:T(8,128)}, u32[]{:S(2)}) copy-start(f32[3,512,2048]{2,1,0:T(8,128)} %copy-done) | copy-start | bytes 37748740 | tf_op jit(solution)/shard_map/while
  478.0 4.8 copy-start
  487.8 12.7 %copy-start.1 = (f32[3,512,2048]{2,1,0:T(8,128)S(1)}, f32[3,512,2048]{2,1,0:T(8,128)}, u32[]{:S(2)}) copy-start(f32[3,512,2048]{2,1,0:T(8,128)} %copy-done) | copy-start | bytes 37748740 | tf_op jit(solution)/shard_map/while
  507.6 4.7 copy-start
  517.2 12.0 %copy-start.1 = (f32[3,512,2048]{2,1,0:T(8,128)S(1)}, f32[3,512,2048]{2,1,0:T(8,128)}, u32[]{:S(2)}) copy-start(f32[3,512,2048]{2,1,0:T(8,128)} %copy-done) | copy-start | bytes 37748740 | tf_op jit(solution)/shard_map/while
  534.4 3.6 copy-start.5
  534.4 3.6 copy-start.6
  534.4 3.6 copy-start.8
  540.9 6.4 copy-start.2
  552.3 10.9 %copy-start.3 = (f32[3,512,2048]{2,1,0:T(8,128)S(1)}, f32[3,512,2048]{2,1,0:T(8,128)}, u32[]{:S(2)}) copy-start(f32[3,512,2048]{2,1,0:T(8,128)} %copy-done.2) | copy-start | bytes 37748740 | tf_op jit(solution)/shard_map/while
  570.9 6.4 copy-start.2
  582.3 10.7 %copy-start.3 = (f32[3,512,2048]{2,1,0:T(8,128)S(1)}, f32[3,512,2048]{2,1,0:T(8,128)}, u32[]{:S(2)}) copy-start(f32[3,512,2048]{2,1,0:T(8,128)} %copy-done.2) | copy-start | bytes 37748740 | tf_op jit(solution)/shard_map/while
  601.3 6.4 copy-start.2
  612.6 11.2 %copy-start.3 = (f32[3,512,2048]{2,1,0:T(8,128)S(1)}, f32[3,512,2048]{2,1,0:T(8,128)}, u32[]{:S(2)}) copy-start(f32[3,512,2048]{2,1,0:T(8,128)} %copy-done.2) | copy-start | bytes 37748740 | tf_op jit(solution)/shard_map/while
  632.3 6.4 copy-start.2
  643.7 11.3 %copy-start.3 = (f32[3,512,2048]{2,1,0:T(8,128)S(1)}, f32[3,512,2048]{2,1,0:T(8,128)}, u32[]{:S(2)}) copy-start(f32[3,512,2048]{2,1,0:T(8,128)} %copy-done.2) | copy-start | bytes 37748740 | tf_op jit(solution)/shard_map/while
  663.1 7.0 copy-start.18
  673.7 1.7 copy-start.16
  673.7 1.8 copy-start.17
  807.7 4.0 copy-start.39
  811.7 4.2 copy-start.13
  819.4 2.8 copy-start.25
  819.4 3.0 copy-start.29
  819.4 3.2 copy-start.28
  819.4 3.3 copy-start.27
  819.4 3.5 copy-start.23
  819.5 3.7 copy-start.26
  819.5 74.6 %copy-start.20 = (f32[1024,768]{1,0:T(8,128)S(1)}, f32[1024,768]{1,0:T(8,128)}, u32[]{:S(2)}) copy-start(f32[1024,768]{1,0:T(8,128)} %copy-done.19) | copy-start | bytes 9437188
  (2 other events, 1.5 us)
Sparse Core Ops, SparseCore 0:
  9.7 44.8 all-gather.5
  56.2 21.5 all-gather.7
  79.4 51.4 all-gather.9
  132.4 50.5 all-gather.11
  366.5 97.0 reduce-scatter.6
  470.3 134.5 reduce-scatter.8
  610.8 159.8 reduce-scatter.10
  819.6 121.8 reduce-scatter.4
